TPU v7x, 256 devices: a whole 4x4x8 slice. The times are simulated.
256 devices in a mesh: tile: 16 (over x, z_hi, core), off: 16 (over z_lo, y).
Axes of the slice: x: 4, y: 4, z: 8 (z_hi: 2, z_lo: 4; z = z_hi * 4 + z_lo), core: 2. Of those that a mesh axis runs over, the one named last changes fastest.
Arguments:
- image_cube: float32 [64, 256, 128, 128], P('off', 'tile'), may hold values from -6 to 6
- time_weight: float32 [256, 128, 128], P('tile'), may hold values from 0.3 to 1
- offset_weight: int32 [64], P('off'), may hold values from 1 to 4
- refine_first: float32 [256, 32], P('tile'), may hold values from -0.375 to 0.375
- refine_second: float32 [128, 16], replicated, may hold values from -0.5 to 0.5
- refine_depth: float32 [128, 16], replicated, may hold values from -0.5 to 0.5
- owner_rows: int32 [32], replicated, may hold values from 0 to 31, each once
Outputs:
- coarse_gradient: float32 [32, 16, 16], P('tile', 'off')
Inputs may be any that keep to these rules, and one draw needn't show every extreme that they name: owner_rows names each of the 32 coarse first-dimension indices exactly once.
All inputs are finite; a program needn't handle non-finite values.
Results may differ from a plain program's by a relative error of at most 0.0003.
Values sent between devices are 32-bit elements; how exact they have to be, the bound alone decides.
A program may use at most 64 MiB of HBM per device.

v0:
```python
import jax
import jax.numpy as jnp
from jax import lax
from jax.sharding import PartitionSpec as P

NH = 64


def shifted(x, axis, by):
    length = lax.axis_size(axis)
    pairs = [(i, i + by) for i in range(length) if 0 <= i + by < length]
    return lax.ppermute(x, axis, pairs)


def contract_coarse(fine_grad, rows_first, second, depth):
    highest = lax.Precision.HIGHEST
    along_depth = jnp.einsum("xyz,zc->xyc", fine_grad, depth, precision=highest)
    along_second = jnp.einsum("xyc,yb->xbc", along_depth, second, precision=highest)
    return jnp.einsum("xbc,xa->abc", along_second, rows_first, precision=highest)


def depth_difference(cube):
    depth_next = jnp.concatenate([cube[..., 1:], jnp.zeros_like(cube[..., :1])], axis=-1)
    return depth_next - cube


def local(
    image_cube, time_weight, offset_weight, refine_first, refine_second, refine_depth, owner_rows
):
    following = shifted(image_cube[0], "off", -1)
    ahead = jnp.concatenate([image_cube[1:], following[None]], axis=0)
    difference = ahead - image_cube
    weights = offset_weight.astype(jnp.float32)[:, None, None, None] * time_weight[None]
    residual = weights * difference
    weighted = weights * residual
    depth_diff = depth_difference(image_cube)
    preceding = shifted(weighted[-1], "off", 1)
    behind = jnp.concatenate([preceding[None], weighted[:-1]], axis=0)
    adjoint = behind - weighted
    fine_grad = jnp.sum(adjoint * depth_diff, axis=0) / NH
    coarse_first = refine_first.shape[1]
    coarse_second = refine_second.shape[1]
    coarse_depth = refine_depth.shape[1]
    selector = (jnp.arange(coarse_first, dtype=jnp.int32)[:, None] == owner_rows[None, :]).astype(
        jnp.float32
    )
    permuted_first = jnp.dot(
        refine_first, selector, precision=lax.Precision.HIGHEST, preferred_element_type=jnp.float32
    )
    slab_width = fine_grad.shape[1] // lax.axis_size("off")
    summed = lax.psum_scatter(fine_grad, "off", scatter_dimension=1, tiled=True)
    second_rows = lax.dynamic_slice_in_dim(
        refine_second, lax.axis_index("off") * slab_width, slab_width, 0
    )
    partial_sum = contract_coarse(summed, permuted_first, second_rows, refine_depth)
    tile_count = lax.axis_size("tile")
    part_count = lax.axis_size("off")
    rows_dev = coarse_first // tile_count
    cols_dev = coarse_second // part_count
    arranged = partial_sum.reshape(tile_count, rows_dev, part_count, cols_dev, coarse_depth)
    arranged = arranged.transpose(0, 2, 1, 3, 4).reshape(
        tile_count * part_count * rows_dev, cols_dev, coarse_depth
    )
    return lax.psum_scatter(arranged, ("tile", "off"), scatter_dimension=0, tiled=True)


def solution(mesh):
    in_specs = (
        P("off", "tile", None, None),
        P("tile", None, None),
        P("off"),
        P("tile", None),
        P(),
        P(),
        P(),
    )
    out_specs = P("tile", "off", None)
    return jax.shard_map(local, mesh=mesh, in_specs=in_specs, out_specs=out_specs, check_vma=False)
```

profile of v0, /device:TPU:1, one launch (start us, length us, event | category | flops | bytes accessed | tf_op | source)
XLA Modules:
  0.0 244.7 jit_solution(15309527696025362374)
XLA Ops:
  6.5 0.0 copy-start.1
  6.6 1.4 slice_bitcast_fusion.1
  8.0 1.6 collective-permute-start
  9.6 23.3 %collective-permute-done = f32[16,128,128]{2,1,0:T(8,128)S(1)} collective-permute-done((f32[16,128,128]{2,1,0:T(8,128)S(1)}, f32[16,128,128]{2,1,0:T(8,128)S(1)}, u32[]{:S(2)}, u32[]{:S(2)}) %collective-permute-start) | collective-permute-done | bytes 1048608 | tf_op jit(solution)/shard_map/ppermute | solution.py:12
  32.9 1.5 multiply_multiply_fusion
  34.5 0.1 slice_bitcast_fusion
  34.6 5.4 %collective-permute-start.1 = (f32[16,128,128]{2,1,0:T(8,128)S(1)}, f32[16,128,128]{2,1,0:T(8,128)S(1)}, u32[]{:S(2)}, u32[]{:S(2)}) collective-permute-start(f32[16,128,128]{2,1,0:T(8,128)S(1)} %slice_bitcast_fusion), channel_id=1, source_target_pairs={{0,1},{1,2},{2,3},{3,4},{4,5},{5,6},{6,7},{7,8},{8,9},{9,10},{10,1... | collective-permute-start | bytes 3145736 | tf_op jit(solution)/shard_map/ppermute | solution.py:12
  39.9 1.1 slice.19
  41.1 1.9 slice.21
  42.9 17.8 %collective-permute-done.1 = f32[16,128,128]{2,1,0:T(8,128)S(1)} collective-permute-done((f32[16,128,128]{2,1,0:T(8,128)S(1)}, f32[16,128,128]{2,1,0:T(8,128)S(1)}, u32[]{:S(2)}, u32[]{:S(2)}) %collective-permute-start.1) | collective-permute-done | bytes 1048608 | tf_op jit(solution)/shard_map/ppermute | solution.py:12
  60.8 1.0 copy-done.2
  61.8 4.3 %fusion.1 = f32[16,128,128]{2,1,0:T(8,128)S(1)} fusion(f32[4,16,128,128]{3,2,1,0:T(8,128)S(1)} %multiply_multiply_fusion, f32[3,16,128,128]{3,2,1,0:T(8,128)} %slice.21, f32[1,16,128,128]{3,2,1,0:T(8,128)} %bitcast.27, f32[4,16,128,128]{3,2,1,0:T(8,128)S(1)} %copy-done.1, f32[4,16,128,127]{3,2,1,0:T(8,128)S(1)} %slice.19), kind=kLoop, calls=%fused_computation.4 | loop fusion | flops 4980736 | bytes 17793024 | tf_op jit(solution)/shard_map/reduce_sum | solution.py:40
  66.1 1.1 broadcast_multiply_fusion
  67.1 0.0 reduce-scatter.3.cloned.1.call-update
  67.2 0.1 fusion.2
  67.3 81.6 %reduce-scatter.3.cloned.1.call-done = f32[16,8,128]{2,1,0:T(8,128)} async-done(((f32[16,128,128]{2,1,0:T(8,128)}), f32[16,8,128]{2,1,0:T(8,128)}) %reduce-scatter.3.cloned.1.call-update) | async-done | bytes 65552 | tf_op jit(solution)/shard_map/reduce_scatter | solution.py:51
  148.9 1.0 fusion.4
  150.0 0.3 convolution_bitcast_fusion
  150.3 0.1 copy.16
  150.4 0.2 fusion.9
  150.7 0.2 copy.17
  150.8 0.1 copy.18
  151.0 86.3 %all-reduce.1 = f32[512,1,16]{2,0,1:T(8,128)S(1)} all-reduce(f32[512,1,16]{2,0,1:T(8,128)S(1)} %bitcast.29), channel_id=3, replica_groups=mesh['tile'=16,'off'=16] {'tile','off'}, use_global_device_ids=true, to_apply=%region_2.0.clone | all-reduce | flops 8192 | bytes 65536
  237.3 0.6 constant_dynamic-slice_fusion
  (18 shorter events, 0.0 us)
Async XLA Ops:
  6.5 143.4 %copy-start = (f32[128,16]{0,1:T(8,128)S(1)}, f32[128,16]{0,1:T(8,128)}, u32[]{:S(2)}) copy-start(f32[128,16]{0,1:T(8,128)} %param.11) | copy-start | bytes 24580
  6.5 26.4 %slice-start = ((f32[4,16,128,128]{3,2,1,0:T(8,128)}), f32[3,16,128,128]{3,2,1,0:T(8,128)S(1)}, s32[]{:S(2)}) async-start(f32[4,16,128,128]{3,2,1,0:T(8,128)} %param.7), calls=%async_computation.2 | async-start | bytes 6291456 | tf_op jit(solution)/shard_map/slice | solution.py:31
  6.5 3.0 %copy-start.7 = (s32[4]{0:T(128)S(1)}, s32[4]{0:T(128)}, u32[]{:S(2)}) copy-start(s32[4]{0:T(128)} %param.9) | copy-start | bytes 52
  6.5 142.4 %reduce-scatter.3.cloned.1.call-start = ((), (), s32[]{:S(2)}) async-start(), calls=%async_computation.1 | async-start | bytes 1114112 | tf_op jit(solution)/shard_map/reduce_scatter | solution.py:51
  6.5 26.4 %copy-start.1 = (f32[4,16,128,128]{3,2,1,0:T(8,128)S(1)}, f32[4,16,128,128]{3,2,1,0:T(8,128)}, u32[]{:S(2)}) copy-start(f32[4,16,128,128]{3,2,1,0:T(8,128)} %param.7) | copy-start | bytes 12582916
  6.6 26.4 %copy-start.3 = (f32[16,128,128]{2,1,0:T(8,128)S(1)}, f32[16,128,128]{2,1,0:T(8,128)}, u32[]{:S(2)}) copy-start(f32[16,128,128]{2,1,0:T(8,128)} %param.8) | copy-start | bytes 3145732
  8.0 24.9 %collective-permute-start = (f32[16,128,128]{2,1,0:T(8,128)S(1)}, f32[16,128,128]{2,1,0:T(8,128)S(1)}, u32[]{:S(2)}, u32[]{:S(2)}) collective-permute-start(f32[16,128,128]{2,1,0:T(8,128)S(1)} %slice_bitcast_fusion.1), channel_id=1, source_target_pairs={{1,0},{2,1},{3,2},{4,3},{5,4},{6,5},{7,6},{8,7},{9,8},{10,9},{11,1... | collective-permute-start | bytes 3145736 | tf_op jit(solution)/shard_map/ppermute | solution.py:12
  34.6 26.2 %collective-permute-start.1 = (f32[16,128,128]{2,1,0:T(8,128)S(1)}, f32[16,128,128]{2,1,0:T(8,128)S(1)}, u32[]{:S(2)}, u32[]{:S(2)}) collective-permute-start(f32[16,128,128]{2,1,0:T(8,128)S(1)} %slice_bitcast_fusion), channel_id=1, source_target_pairs={{0,1},{1,2},{2,3},{3,4},{4,5},{5,6},{6,7},{7,8},{8,9},{9,10},{10,1... | collective-permute-start | bytes 3145736 | tf_op jit(solution)/shard_map/ppermute | solution.py:12
  60.8 1.0 copy-start.2
  61.8 5.4 %copy-start.5 = (f32[16,32]{1,0:T(8,128)S(1)}, f32[16,32]{1,0:T(8,128)}, u32[]{:S(2)}) copy-start(f32[16,32]{1,0:T(8,128)} %param.10) | copy-start | bytes 6148
  61.8 5.4 %copy-start.6 = (s32[32]{0:T(128)S(1)}, s32[32]{0:T(128)}, u32[]{:S(2)}) copy-start(s32[32]{0:T(128)} %param.13) | copy-start | bytes 388
  61.8 87.2 %copy-start.4 = (f32[128,16]{0,1:T(8,128)S(1)}, f32[128,16]{0,1:T(8,128)}, u32[]{:S(2)}) copy-start(f32[128,16]{0,1:T(8,128)} %param.12) | copy-start | bytes 24580
Sparse Core Ops, SparseCore 0:
  67.3 81.6 reduce-scatter.2
where the time goes:
time: 245 us
  waiting for transfers between devices  123 us (50%)
  blocking collectives  86.3 us (35%)
  between operations  13.6 us (6%)
  starting transfers between devices  6.93 us (3%)
  other arithmetic  6.87 us (3%)
  local copies, waits for them, and re-layouts  6.55 us (3%)
    unnamed x1, blocking collectives  86.3 us
    reduce_scatter x1, waiting for transfers between devices, local(): summed = lax.psum_scatter(fine_grad, 'off', scatter_dimension=1, tiled=True)  81.6 us
    ppermute x2, waiting for transfers between devices, shifted(): return lax.ppermute(x, axis, pairs)  41.1 us
    ppermute x2, starting transfers between devices, shifted(): return lax.ppermute(x, axis, pairs)  6.93 us
  transfers between devices with their start and end apart: 3, of which 3 were waited for; matrix products, arithmetic and copies ran while one was open for 1% of the time, Pallas kernels for 0%

commit v1 on v0

v1 whole, which is shorter than its diff:
```python
import functools

import jax
import jax.numpy as jnp
from jax import lax
from jax.experimental import pallas as pl
from jax.experimental.pallas import tpu as pltpu
from jax.sharding import PartitionSpec as P

MESH = pl.DeviceIdType.MESH
F32 = jnp.float32
BF16 = jnp.bfloat16
HIGHEST = lax.Precision.HIGHEST

NH = 64
LOCAL = 4
ROWS = 16
HALF = 8
N = 128
COARSE = 16
OFFS = 16
TILES = 16


def iota(shape, axis):
    return lax.broadcasted_iota(jnp.int32, shape, axis)


def dot(a, b):
    return jnp.dot(a, b, preferred_element_type=F32)


def split(x):
    high = x.astype(BF16)
    return high, (x - high.astype(F32)).astype(BF16)


def kernel(
    cube, time, weight, first, second, depth, owner, out,
    cube_v, time_v, weight_v, first_v, second_v, depth_v, owner_v,
    before, after, weight_before, grad, place, expand, spread,
    send1, recv1, send2, recv2,
    load_sem, up_send, up_recv, down_send, down_recv, word_send, word_recv,
    s1_send, s1_recv, s2_send, s2_recv,
):
    tile = lax.axis_index("tile")
    off = lax.axis_index("off")
    has_after = off < OFFS - 1
    has_before = off > 0

    barrier = pltpu.get_barrier_semaphore()
    for j in range(1, OFFS):
        pl.semaphore_signal(
            barrier, inc=1, device_id=(tile, lax.rem(off + j, OFFS)), device_id_type=MESH
        )
    for j in range(1, TILES):
        pl.semaphore_signal(
            barrier, inc=1, device_id=(lax.rem(tile + j, TILES), off), device_id_type=MESH
        )
    loads = [
        pltpu.make_async_copy(src, dst, load_sem.at[i])
        for i, (src, dst) in enumerate(
            [
                (weight, weight_v),
                (first, first_v),
                (second, second_v),
                (depth, depth_v),
                (owner, owner_v),
                (time, time_v),
                (cube, cube_v),
            ]
        )
    ]
    for load in loads:
        load.start()
    pl.semaphore_wait(barrier, OFFS - 1 + TILES - 1)

    def up(k):
        return pltpu.make_async_remote_copy(
            src_ref=cube.at[LOCAL - 1, HALF + k],
            dst_ref=before.at[k],
            send_sem=up_send.at[k],
            recv_sem=up_recv.at[k],
            device_id=(tile, off + 1),
            device_id_type=MESH,
        )

    def down(k):
        return pltpu.make_async_remote_copy(
            src_ref=cube.at[0, k],
            dst_ref=after.at[k],
            send_sem=down_send.at[k],
            recv_sem=down_recv.at[k],
            device_id=(tile, off - 1),
            device_id_type=MESH,
        )

    word = pltpu.make_async_remote_copy(
        src_ref=weight,
        dst_ref=weight_before,
        send_sem=word_send,
        recv_sem=word_recv,
        device_id=(tile, off + 1),
        device_id_type=MESH,
    )

    @pl.when(has_after)
    def _():
        word.start()
        for k in range(HALF):
            up(k).start()

    @pl.when(has_before)
    def _():
        for k in range(HALF):
            down(k).start()

    for load in loads:
        load.wait()

    lane = iota((N, N), 1)
    second_high, second_low = split(second_v[...])
    left = jnp.concatenate(
        [
            jnp.concatenate([second_high, second_high], axis=1),
            jnp.concatenate([second_low, jnp.zeros_like(second_low)], axis=1),
        ],
        axis=0,
    )
    depth_wide = jnp.transpose(jnp.concatenate([depth_v[...]] * (N // COARSE), axis=0))
    for q in range(4):
        for p in range(2):
            part = jnp.where(lane // COARSE == 2 * q + p, depth_wide, 0.0)
            high, low = split(part)
            place[q, p * N : (p + 1) * N, :N] = high
            place[q, p * N : (p + 1) * N, N:] = low
    owner_rows = jnp.broadcast_to(owner_v[...].astype(F32), (N, 32))
    for r in range(2):
        pick = (iota((TILES, 32), 1) == 2 * iota((TILES, 32), 0) + r).astype(F32)
        owned = lax.dot_general(
            pick, owner_rows, (((1,), (1,)), ((), ())), precision=HIGHEST,
            preferred_element_type=F32,
        )
        select = (owned[:, :32] == iota((TILES, 32), 1).astype(F32)).astype(F32)
        chosen = lax.dot_general(
            select, first_v[...], (((1,), (1,)), ((), ())), precision=HIGHEST,
            preferred_element_type=F32,
        )
        for h in range(2):
            group = iota((ROWS, N), 1) // COARSE
            row = lax.rem(group, 2) * HALF + h * 4 + group // 2
            where = (row == iota((ROWS, N), 0)).astype(F32)
            expand[r, h] = jnp.dot(chosen, where, precision=HIGHEST, preferred_element_type=F32)
    spread[...] = (
        iota((2 * N, N), 1) == iota((2 * N, N), 0) // N * COARSE + lax.rem(iota((2 * N, N), 0), COARSE)
    ).astype(F32).astype(BF16)

    own = weight_v[...].astype(F32)
    own = own * own
    scale = [
        jnp.sum(jnp.where(iota((1, LOCAL), 1) == h, own, 0.0), axis=1, keepdims=True)
        for h in range(LOCAL)
    ]

    def term(difference, factor):
        last = iota(difference.shape, 1) == N - 1
        following = jnp.where(last, 0.0, pltpu.roll(difference, N - 1, 1))
        return (factor * difference) * (following - difference)

    STEP = 32

    @pl.loop(0, ROWS)
    def _(x):
        for y in range(0, N, STEP):
            rows = pl.ds(y, STEP)
            planes = [cube_v[h, x, rows, :] for h in range(LOCAL)]
            total = term(planes[1] - planes[0], scale[0])
            for h in range(1, LOCAL - 1):
                total += term(planes[h + 1] - planes[h], scale[h])
            grad[x, rows, :] = total
            w = time_v[x, rows, :]
            time_v[x, rows, :] = w * w * (1.0 / NH)

    @pl.when(jnp.logical_not(has_after))
    def _():
        @pl.loop(0, HALF)
        def _(k):
            after[k] = jnp.zeros((N, N), F32)
            for y in range(0, N, STEP):
                rows = pl.ds(y, STEP)
                grad[HALF + k, rows, :] += term(-cube_v[LOCAL - 1, HALF + k, rows, :], scale[3])

    @pl.when(jnp.logical_not(has_before))
    def _():
        weight_before[...] = jnp.zeros((1, LOCAL), jnp.int32)

        @pl.loop(0, HALF)
        def _(k):
            before[k] = jnp.zeros((N, N), F32)

    @pl.when(has_before)
    def _():
        word.wait_recv()

    theirs = weight_before[...].astype(F32)
    theirs = theirs * theirs
    scale_before = jnp.sum(
        jnp.where(iota((1, LOCAL), 1) == LOCAL - 1, theirs, 0.0), axis=1, keepdims=True
    )

    for h in range(2):

        def step(q, coarse, h=h):
            k = h * 4 + q

            @pl.when(has_after)
            def _():
                down(k).wait_recv()

            @pl.when(has_before)
            def _():
                up(k).wait_recv()

            low_rows = time_v[k] * (grad[k] + term(after[k] - cube_v[LOCAL - 1, k], scale[3]))
            high_rows = time_v[HALF + k] * (
                grad[HALF + k] + term(cube_v[0, HALF + k] - before[k], scale_before)
            )
            a_high, a_low = split(low_rows)
            b_high, b_low = split(high_rows)
            right = jnp.concatenate(
                [
                    jnp.concatenate([a_high, b_high], axis=1),
                    jnp.concatenate([a_low, b_low], axis=1),
                ],
                axis=0,
            )
            along = dot(left, right)
            along = along[:COARSE] + along[COARSE:]
            both = dot(jnp.concatenate(split(along), axis=0), place[q])
            return coarse + (
                both[:COARSE, :N] + (both[:COARSE, N:] + both[COARSE:, :N])
            )

        coarse = lax.fori_loop(0, 4, step, jnp.zeros((COARSE, N), F32))
        for b in range(COARSE):
            send1[b, h : h + 1, :] = coarse[b : b + 1]

    def to_off(j):
        peer = lax.rem(off + j, OFFS)
        return pltpu.make_async_remote_copy(
            src_ref=send1.at[peer],
            dst_ref=recv1.at[j],
            send_sem=s1_send,
            recv_sem=s1_recv,
            device_id=(tile, peer),
            device_id_type=MESH,
        )

    for j in range(1, OFFS):
        to_off(j).start()
    recv1[0] = send1[off]
    pltpu.make_async_copy(
        recv1.at[pl.ds(1, OFFS - 1)], recv1.at[pl.ds(1, OFFS - 1)], s1_recv
    ).wait()
    summed = jnp.sum(recv1[...], axis=0)
    lhs = jnp.concatenate(
        [
            expand[r, 0] * summed[0:1, :] + expand[r, 1] * summed[1:2, :]
            for r in range(2)
        ],
        axis=1,
    )
    rows = dot(jnp.concatenate(split(lhs), axis=0), spread[...])
    rows = rows[:TILES] + rows[TILES:]
    for t in range(TILES):
        send2[t, :, :] = rows[t : t + 1]

    def to_tile(j):
        peer = lax.rem(tile + j, TILES)
        return pltpu.make_async_remote_copy(
            src_ref=send2.at[peer],
            dst_ref=recv2.at[j],
            send_sem=s2_send,
            recv_sem=s2_recv,
            device_id=(peer, off),
            device_id_type=MESH,
        )

    for j in range(1, TILES):
        to_tile(j).start()
    recv2[0] = send2[tile]
    pltpu.make_async_copy(
        recv2.at[pl.ds(1, TILES - 1)], recv2.at[pl.ds(1, TILES - 1)], s2_recv
    ).wait()
    result = jnp.sum(recv2[...], axis=0)
    for r in range(2):
        out[r, :, :] = result[:, r * COARSE : (r + 1) * COARSE]

    pltpu.make_async_copy(
        send1.at[pl.ds(0, OFFS - 1)], send1.at[pl.ds(0, OFFS - 1)], s1_send
    ).wait()
    pltpu.make_async_copy(
        send2.at[pl.ds(0, TILES - 1)], send2.at[pl.ds(0, TILES - 1)], s2_send
    ).wait()

    @pl.when(has_after)
    def _():
        word.wait_send()
        for k in range(HALF):
            up(k).wait_send()

    @pl.when(has_before)
    def _():
        for k in range(HALF):
            down(k).wait_send()


def local(cube, time, weight, first, second, depth, owner):
    hbm = pl.BlockSpec(memory_space=pltpu.HBM)
    dma = pltpu.SemaphoreType.DMA
    return pl.pallas_call(
        kernel,
        out_shape=jax.ShapeDtypeStruct((2, 1, COARSE), F32),
        in_specs=[hbm] * 7,
        out_specs=pl.BlockSpec(memory_space=pltpu.VMEM),
        scratch_shapes=[
            pltpu.VMEM((LOCAL, ROWS, N, N), F32),
            pltpu.VMEM((ROWS, N, N), F32),
            pltpu.VMEM((1, LOCAL), jnp.int32),
            pltpu.VMEM((ROWS, 32), F32),
            pltpu.VMEM((COARSE, N), F32),
            pltpu.VMEM((COARSE, N), F32),
            pltpu.VMEM((1, 32), jnp.int32),
            pltpu.VMEM((HALF, N, N), F32),
            pltpu.VMEM((HALF, N, N), F32),
            pltpu.VMEM((1, LOCAL), jnp.int32),
            pltpu.VMEM((ROWS, N, N), F32),
            pltpu.VMEM((4, 2 * N, 2 * N), BF16),
            pltpu.VMEM((2, 2, TILES, N), F32),
            pltpu.VMEM((2 * N, N), BF16),
            pltpu.VMEM((COARSE, 2, N), F32),
            pltpu.VMEM((OFFS, 2, N), F32),
            pltpu.VMEM((TILES, 1, N), F32),
            pltpu.VMEM((TILES, 1, N), F32),
            dma((7,)),
            dma((HALF,)),
            dma((HALF,)),
            dma((HALF,)),
            dma((HALF,)),
            dma,
            dma,
            dma,
            dma,
            dma,
            dma,
        ],
        compiler_params=pltpu.CompilerParams(
            collective_id=0, has_side_effects=True, vmem_limit_bytes=32 * 1024 * 1024
        ),
    )(
        cube,
        time,
        weight.reshape(1, LOCAL),
        first,
        second.T,
        depth.T,
        owner.reshape(1, 32),
    )


def solution(mesh):
    in_specs = (
        P("off", "tile", None, None),
        P("tile", None, None),
        P("off"),
        P("tile", None),
        P(),
        P(),
        P(),
    )
    out_specs = P("tile", "off", None)
    return jax.shard_map(local, mesh=mesh, in_specs=in_specs, out_specs=out_specs, check_vma=False)
```

time: 245 us -> 43 us (0.18)
  waiting for transfers between devices: 123 us -> 0 us
  blocking collectives: 86.3 us -> 0 us
  Pallas kernels: 0 us -> 35.4 us
  between operations: 13.6 us -> 0.02 us
  starting transfers between devices: 6.93 us -> 0 us
  other arithmetic: 6.87 us -> 0 us
    unnamed x1 -> x0, blocking collectives: 86.3 us -> none
    reduce_scatter x1 -> x0, waiting for transfers between devices: 81.6 us -> none  [local(): summed = lax.psum_scatter(fine_grad, 'off', scatter_dimension=1, tiled=True)]
    ppermute x2 -> x0, waiting for transfers between devices: 41.1 us -> none  [shifted(): return lax.ppermute(x, axis, pairs)]
    pallas_call x0 -> x1, Pallas kernels: none -> 35.4 us  [local(): pl.pallas_call(kernel, out_shape=jax.ShapeDtypeStruct((2, 1, COARSE), F32...]
    ppermute x2 -> x0, starting transfers between devices: 6.93 us -> none  [shifted(): return lax.ppermute(x, axis, pairs)]
    unnamed x17 -> x15, local copies, waits for them, and re-layouts: 1.59 us -> 7.37 us
    reduce_sum x1 -> x0, other arithmetic: 4.3 us -> none  [local(): fine_grad = jnp.sum(adjoint * depth_diff, axis=0) / NH]
    slice x4 -> x0, local copies, waits for them, and re-layouts: 3.01 us -> none  [the longest x1 1.86 us: local(): behind = jnp.concatenate([preceding[None], weighted[:-1]], axis=0)]
  transfers between devices with their start and end apart: 3 -> 0, of which waited for: 3 -> 0; matrix products, arithmetic and copies ran while one was open for 1% -> 0% of each run, Pallas kernels for 0% -> 0%
where the time goes in v1:
time: 43 us; the launch traced here: 42.7 us
  Pallas kernels  35.4 us (82%)
  local copies, waits for them, and re-layouts  7.37 us (17%)
    pallas_call x1, Pallas kernels, local(): pl.pallas_call(kernel, out_shape=jax.ShapeDtypeStruct((2, 1, COARSE), F32...  35.4 us
    unnamed x15, local copies, waits for them, and re-layouts  7.37 us

profile of v1, /device:TPU:1, one launch (start us, length us, event | category | flops | bytes accessed | tf_op | source)
XLA Modules:
  0.0 42.7 jit_solution(18226303324232980702)
XLA Ops:
  0.0 0.0 copy-start
  0.0 2.2 %copy-done = f32[4,16,128,128]{3,2,1,0:T(8,128)S(1)} copy-done((f32[4,16,128,128]{3,2,1,0:T(8,128)S(1)}, f32[4,16,128,128]{3,2,1,0:T(8,128)}, u32[]{:S(2)}) %copy-start) | copy-done | bytes 4194328
  2.2 0.0 copy-start.1
  2.2 1.2 %copy-done.1 = f32[16,128,128]{2,1,0:T(8,128)S(1)} copy-done((f32[16,128,128]{2,1,0:T(8,128)S(1)}, f32[16,128,128]{2,1,0:T(8,128)}, u32[]{:S(2)}) %copy-start.1) | copy-done | bytes 1048600
  3.4 0.0 copy-start.2
  3.4 0.7 %copy-done.2 = f32[16,32]{1,0:T(8,128)S(1)} copy-done((f32[16,32]{1,0:T(8,128)S(1)}, f32[16,32]{1,0:T(8,128)}, u32[]{:S(2)}) %copy-start.2) | copy-done | bytes 2072
  4.1 0.0 copy-start.3
  4.1 0.7 %copy-done.3 = f32[128,16]{0,1:T(8,128)S(1)} copy-done((f32[128,16]{0,1:T(8,128)S(1)}, f32[128,16]{0,1:T(8,128)}, u32[]{:S(2)}) %copy-start.3) | copy-done | bytes 8216
  4.8 0.0 copy-start.4
  4.8 0.7 %copy-done.4 = f32[128,16]{0,1:T(8,128)S(1)} copy-done((f32[128,16]{0,1:T(8,128)S(1)}, f32[128,16]{0,1:T(8,128)}, u32[]{:S(2)}) %copy-start.4) | copy-done | bytes 8216
  5.5 0.0 copy-start.5
  5.5 0.7 %copy-done.5 = s32[4]{0:T(128)S(1)} copy-done((s32[4]{0:T(128)S(1)}, s32[4]{0:T(128)}, u32[]{:S(2)}) %copy-start.5) | copy-done | bytes 40
  6.2 0.0 copy-start.6
  6.2 0.7 %copy-done.6 = s32[32]{0:T(128)S(1)} copy-done((s32[32]{0:T(128)S(1)}, s32[32]{0:T(128)}, u32[]{:S(2)}) %copy-start.6) | copy-done | bytes 152
  6.8 35.4 %shard_map.73 = f32[2,1,16]{2,1,0:T(1,128)S(1)} custom-call(f32[4,16,128,128]{3,2,1,0:T(8,128)S(1)} %copy-done, f32[16,128,128]{2,1,0:T(8,128)S(1)} %copy-done.1, s32[1,4]{1,0:T(1,128)S(1)} %bitcast.6, f32[16,32]{1,0:T(8,128)S(1)} %copy-done.2, f32[16,128]{1,0:T(8,128)S(1)} %bitcast.4, f32[16,128]{1,0:T(8,128)S(1)} %bitcast.5, s32[1,32]{1,0:T(1,128)S(1)} %bitcast.7), custom_call_target="tpu_custom_call" | custom-call | tf_op jit(solution)/shard_map/pallas_call | solution.py:321
  42.2 0.6 %copy.9 = f32[2,1,16]{2,1,0:T(1,128)} copy(f32[2,1,16]{2,1,0:T(1,128)S(1)} %shard_map.73) | data formatting | bytes 256
Async XLA Ops:
  0.0 2.2 %copy-start = (f32[4,16,128,128]{3,2,1,0:T(8,128)S(1)}, f32[4,16,128,128]{3,2,1,0:T(8,128)}, u32[]{:S(2)}) copy-start(f32[4,16,128,128]{3,2,1,0:T(8,128)} %cube.1) | copy-start | bytes 12582916
  2.2 1.2 %copy-start.1 = (f32[16,128,128]{2,1,0:T(8,128)S(1)}, f32[16,128,128]{2,1,0:T(8,128)}, u32[]{:S(2)}) copy-start(f32[16,128,128]{2,1,0:T(8,128)} %time.1) | copy-start | bytes 3145732
  3.4 0.7 %copy-start.2 = (f32[16,32]{1,0:T(8,128)S(1)}, f32[16,32]{1,0:T(8,128)}, u32[]{:S(2)}) copy-start(f32[16,32]{1,0:T(8,128)} %first.1) | copy-start | bytes 6148
  4.1 0.7 %copy-start.3 = (f32[128,16]{0,1:T(8,128)S(1)}, f32[128,16]{0,1:T(8,128)}, u32[]{:S(2)}) copy-start(f32[128,16]{0,1:T(8,128)} %param.11) | copy-start | bytes 24580
  4.8 0.7 %copy-start.4 = (f32[128,16]{0,1:T(8,128)S(1)}, f32[128,16]{0,1:T(8,128)}, u32[]{:S(2)}) copy-start(f32[128,16]{0,1:T(8,128)} %param.12) | copy-start | bytes 24580
  5.5 0.7 %copy-start.5 = (s32[4]{0:T(128)S(1)}, s32[4]{0:T(128)}, u32[]{:S(2)}) copy-start(s32[4]{0:T(128)} %param.9) | copy-start | bytes 52
  6.2 0.7 %copy-start.6 = (s32[32]{0:T(128)S(1)}, s32[32]{0:T(128)}, u32[]{:S(2)}) copy-start(s32[32]{0:T(128)} %param.13) | copy-start | bytes 388

commit v2 on v1

v2 whole, which is shorter than its diff:
```python
import jax
import jax.numpy as jnp
from jax import lax
from jax.experimental import pallas as pl
from jax.experimental.pallas import tpu as pltpu
from jax.sharding import PartitionSpec as P

MESH = pl.DeviceIdType.MESH
F32 = jnp.float32
BF16 = jnp.bfloat16
HIGHEST = lax.Precision.HIGHEST

NH = 64
LOCAL = 4
ROWS = 16
HALF = 8
N = 128
COARSE = 16
FIRST = 32
WIDE = FIRST * COARSE
OFFS = 16
GROUP = 16
STRIP = 32


def iota(shape, axis):
    return lax.broadcasted_iota(jnp.int32, shape, axis)


def dot(a, b):
    return jnp.dot(a, b, preferred_element_type=F32)


def split(x):
    high = x.astype(BF16)
    return high, (x - high.astype(F32)).astype(BF16)


def term(difference, factor):
    last = iota(difference.shape, 1) == N - 1
    following = jnp.where(last, 0.0, pltpu.roll(difference, N - 1, 1))
    return (factor * difference) * (following - difference)


def pick(row, index):
    return jnp.sum(jnp.where(iota(row.shape, 1) == index, row, 0.0), axis=1, keepdims=True)


def hops(size, step):
    return min(step, size - step)


PLANE = sorted(
    [(dx, dy) for dx in range(4) for dy in range(4) if dx or dy],
    key=lambda d: (-hops(4, d[0]) - hops(4, d[1]), d),
)
LINE = sorted(
    [(dz, dc) for dz in range(8) for dc in range(2) if dz or dc],
    key=lambda d: (-hops(8, d[0]) - d[1], d),
)


def kernel(
    cube, time, weight, first, second, depth, owner, out,
    cube_v, time_v, weight_v, first_v, second_v, depth_v, owner_v,
    before, after, weight_before, grad, chosen, place,
    send1, recv1, send2, recv2,
    load_sem, up_send, up_recv, down_send, down_recv, word_send, word_recv,
    s1_send, s1_recv, s2_send, s2_recv, near_sem, far_sem, core_sem,
):
    tile = lax.axis_index("tile")
    off = lax.axis_index("off")
    x, z_high, core = lax.div(tile, 4), lax.rem(lax.div(tile, 2), 2), lax.rem(tile, 2)
    z_low, y = lax.div(off, 4), lax.rem(off, 4)
    z = z_high * 4 + z_low
    has_after = off < OFFS - 1
    has_before = off > 0

    def around(dx=0, dy=0, dz=0, dc=0):
        to_x, to_y = lax.rem(x + dx, 4), lax.rem(y + dy, 4)
        to_z, to_core = lax.rem(z + dz, 8), lax.rem(core + dc, 2)
        return (to_x * 4 + lax.div(to_z, 4) * 2 + to_core, lax.rem(to_z, 4) * 4 + to_y)

    def signal(semaphore, device):
        pl.semaphore_signal(semaphore, inc=1, device_id=device, device_id_type=MESH)

    beside = [dict(dy=1), dict(dy=3), dict(dz=1), dict(dz=7), dict(dx=1), dict(dx=3), dict(dc=1)]
    beyond = [dict(dy=2), dict(dz=2), dict(dz=6), dict(dx=2)]
    barrier = pltpu.get_barrier_semaphore()
    turns_after = jnp.logical_and(y == 3, has_after)
    turns_before = jnp.logical_and(y == 0, has_before)

    @pl.when(turns_after)
    def _():
        signal(barrier, (tile, off + 1))

    @pl.when(turns_before)
    def _():
        signal(barrier, (tile, off - 1))

    for d in beside:
        signal(barrier, around(**d))
    loads = [
        pltpu.make_async_copy(src, dst, load_sem.at[i])
        for i, (src, dst) in enumerate(
            [
                (weight, weight_v),
                (first, first_v),
                (second, second_v),
                (depth, depth_v),
                (owner, owner_v),
                (time, time_v),
                (cube, cube_v),
            ]
        )
    ]
    for load in loads[:5]:
        load.start()
    extra = turns_after.astype(jnp.int32) + turns_before.astype(jnp.int32)
    pl.semaphore_wait(barrier, len(beside) + extra)

    def up(k):
        return pltpu.make_async_remote_copy(
            src_ref=cube.at[LOCAL - 1, HALF + k],
            dst_ref=before.at[k],
            send_sem=up_send.at[k],
            recv_sem=up_recv.at[k],
            device_id=(tile, off + 1),
            device_id_type=MESH,
        )

    def down(k):
        return pltpu.make_async_remote_copy(
            src_ref=cube.at[0, k],
            dst_ref=after.at[k],
            send_sem=down_send.at[k],
            recv_sem=down_recv.at[k],
            device_id=(tile, off - 1),
            device_id_type=MESH,
        )

    word = pltpu.make_async_remote_copy(
        src_ref=weight,
        dst_ref=weight_before,
        send_sem=word_send,
        recv_sem=word_recv,
        device_id=(tile, off + 1),
        device_id_type=MESH,
    )

    @pl.when(has_after)
    def _():
        word.start()
        for k in range(HALF):
            up(k).start()

    @pl.when(has_before)
    def _():
        for k in range(HALF):
            down(k).start()

    for d in beside:
        signal(near_sem, around(**d))
    for load in loads[5:]:
        load.start()
    for load in loads[:5]:
        load.wait()

    rows = [second_v[b : b + 1, :] for q in range(4) for b in range(q, COARSE, 4)]
    second_high, second_low = split(jnp.concatenate(rows, axis=0))
    left = jnp.concatenate(
        [
            jnp.concatenate([second_high, second_high], axis=1),
            jnp.concatenate([second_low, jnp.zeros_like(second_low)], axis=1),
        ],
        axis=0,
    )

    unit = (iota((FIRST, WIDE), 0) == iota((FIRST, WIDE), 1) // COARSE).astype(F32)
    owners = jnp.dot(
        jnp.broadcast_to(owner_v[...].astype(F32), (8, FIRST)), unit,
        precision=HIGHEST, preferred_element_type=F32,
    )
    owned = (iota((FIRST, WIDE), 0).astype(F32) == owners[0:1]).astype(F32)
    chosen[...] = jnp.dot(first_v[...], owned, precision=HIGHEST, preferred_element_type=F32)
    depth_wide = jnp.transpose(jnp.concatenate([depth_v[...]] * (N // COARSE), axis=0))

    @pl.loop(0, HALF)
    def _(k):
        for p in range(2):
            row = chosen[pl.ds(p * HALF + k, 1), :]
            for g in range(WIDE // N):
                high, low = split(depth_wide * row[:, g * N : (g + 1) * N])
                place[k, p * N : (p + 1) * N, g * N : (g + 1) * N] = high
                place[k, p * N : (p + 1) * N, WIDE + g * N : WIDE + (g + 1) * N] = low

    pl.semaphore_wait(near_sem, len(beside))
    for d in beyond:
        signal(far_sem, around(**d))

    own = weight_v[...].astype(F32)
    scale = [pick(own * own, h) for h in range(LOCAL)]

    for load in loads[5:]:
        load.wait()

    @pl.loop(0, ROWS)
    def _(r):
        for s in range(0, N, STRIP):
            strip = pl.ds(s, STRIP)
            planes = [cube_v[h, r, strip, :] for h in range(LOCAL)]
            total = term(planes[1] - planes[0], scale[0])
            for h in range(1, LOCAL - 1):
                total += term(planes[h + 1] - planes[h], scale[h])
            grad[r, strip, :] = total
            w = time_v[r, strip, :]
            time_v[r, strip, :] = w * w * (1.0 / NH)

    pl.semaphore_wait(far_sem, len(beyond))
    signal(core_sem, around(dc=1))

    @pl.when(jnp.logical_not(has_after))
    def _():
        @pl.loop(0, HALF)
        def _(k):
            after[k] = jnp.zeros((N, N), F32)
            for s in range(0, N, STRIP):
                strip = pl.ds(s, STRIP)
                grad[HALF + k, strip, :] += term(
                    -cube_v[LOCAL - 1, HALF + k, strip, :], scale[LOCAL - 1]
                )

    @pl.when(jnp.logical_not(has_before))
    def _():
        weight_before[...] = jnp.zeros((1, LOCAL), jnp.int32)

        @pl.loop(0, HALF)
        def _(k):
            before[k] = jnp.zeros((N, N), F32)

    @pl.when(has_before)
    def _():
        word.wait_recv()

    theirs = weight_before[...].astype(F32)
    scale_before = pick(theirs * theirs, LOCAL - 1)

    def step(k, coarse):
        @pl.when(has_after)
        def _():
            down(k).wait_recv()

        @pl.when(has_before)
        def _():
            up(k).wait_recv()

        low_rows = time_v[k] * (grad[k] + term(after[k] - cube_v[LOCAL - 1, k], scale[LOCAL - 1]))
        high_rows = time_v[HALF + k] * (
            grad[HALF + k] + term(cube_v[0, HALF + k] - before[k], scale_before)
        )
        a_high, a_low = split(low_rows)
        b_high, b_low = split(high_rows)
        right = jnp.concatenate(
            [
                jnp.concatenate([a_high, b_high], axis=1),
                jnp.concatenate([a_low, b_low], axis=1),
            ],
            axis=0,
        )
        along = dot(left, right)
        along = along[:COARSE] + along[COARSE:]
        both = dot(jnp.concatenate(split(along), axis=0), place[k])
        both = both[:COARSE] + both[COARSE:]
        return coarse + (both[:, :WIDE] + both[:, WIDE:])

    pl.semaphore_wait(core_sem, 1)
    coarse = lax.fori_loop(0, HALF, step, jnp.zeros((COARSE, WIDE), F32))
    for to_x in range(4):
        for to_y in range(4):
            send1[to_x * 4 + to_y] = coarse[to_y * 4 : to_y * 4 + 4, to_x * N : (to_x + 1) * N]

    def to_plane(dx, dy):
        index = lax.rem(x + dx, 4) * 4 + lax.rem(y + dy, 4)
        return pltpu.make_async_remote_copy(
            src_ref=send1.at[index],
            dst_ref=recv1.at[dx * 4 + dy],
            send_sem=s1_send,
            recv_sem=s1_recv,
            device_id=around(dx=dx, dy=dy),
            device_id_type=MESH,
        )

    for d in PLANE:
        to_plane(*d).start()
    recv1[0] = send1[x * 4 + y]
    landed = recv1.at[pl.ds(1, GROUP - 1)]
    pltpu.make_async_copy(landed, landed, s1_recv).wait()
    summed = jnp.sum(recv1[...], axis=0)
    for q in range(4):
        send2[q] = summed[q : q + 1]

    def to_line(dz, dc):
        index = lax.rem(z + dz, 4)
        return pltpu.make_async_remote_copy(
            src_ref=send2.at[index],
            dst_ref=recv2.at[dz * 2 + dc],
            send_sem=s2_send,
            recv_sem=s2_recv,
            device_id=around(dz=dz, dc=dc),
            device_id_type=MESH,
        )

    for d in LINE:
        to_line(*d).start()
    recv2[0] = send2[z_low]
    landed = recv2.at[pl.ds(1, GROUP - 1)]
    pltpu.make_async_copy(landed, landed, s2_recv).wait()
    result = jnp.sum(recv2[...], axis=0)
    mine = z_high * 2 + core
    result = pltpu.roll(result, lax.rem(4 - mine, 4) * (2 * COARSE), 1)
    for r in range(2):
        out[r] = result[:, r * COARSE : (r + 1) * COARSE]

    left1 = send1.at[pl.ds(0, GROUP - 1)]
    pltpu.make_async_copy(left1, left1, s1_send).wait()
    left2 = recv2.at[pl.ds(0, GROUP - 1)]
    pltpu.make_async_copy(left2, left2, s2_send).wait()

    @pl.when(has_after)
    def _():
        word.wait_send()
        for k in range(HALF):
            up(k).wait_send()

    @pl.when(has_before)
    def _():
        for k in range(HALF):
            down(k).wait_send()


def local(cube, time, weight, first, second, depth, owner):
    hbm = pl.BlockSpec(memory_space=pltpu.HBM)
    dma = pltpu.SemaphoreType.DMA
    return pl.pallas_call(
        kernel,
        out_shape=jax.ShapeDtypeStruct((2, 1, COARSE), F32),
        in_specs=[hbm] * 7,
        out_specs=pl.BlockSpec(memory_space=pltpu.VMEM),
        scratch_shapes=[
            pltpu.VMEM((LOCAL, ROWS, N, N), F32),
            pltpu.VMEM((ROWS, N, N), F32),
            pltpu.VMEM((1, LOCAL), jnp.int32),
            pltpu.VMEM((ROWS, FIRST), F32),
            pltpu.VMEM((COARSE, N), F32),
            pltpu.VMEM((COARSE, N), F32),
            pltpu.VMEM((1, FIRST), jnp.int32),
            pltpu.VMEM((HALF, N, N), F32),
            pltpu.VMEM((HALF, N, N), F32),
            pltpu.VMEM((1, LOCAL), jnp.int32),
            pltpu.VMEM((ROWS, N, N), F32),
            pltpu.VMEM((ROWS, WIDE), F32),
            pltpu.VMEM((HALF, 2 * N, 2 * WIDE), BF16),
            pltpu.VMEM((GROUP, 4, N), F32),
            pltpu.VMEM((GROUP, 4, N), F32),
            pltpu.VMEM((4, 1, N), F32),
            pltpu.VMEM((GROUP, 1, N), F32),
            dma((7,)),
            dma((HALF,)),
            dma((HALF,)),
            dma((HALF,)),
            dma((HALF,)),
            dma,
            dma,
            dma,
            dma,
            dma,
            dma,
            pltpu.SemaphoreType.REGULAR,
            pltpu.SemaphoreType.REGULAR,
            pltpu.SemaphoreType.REGULAR,
        ],
        compiler_params=pltpu.CompilerParams(
            collective_id=0, has_side_effects=True, vmem_limit_bytes=60 * 1024 * 1024
        ),
    )(
        cube,
        time,
        weight.reshape(1, LOCAL),
        first,
        second.T,
        depth.T,
        owner.reshape(1, FIRST),
    )


def solution(mesh):
    in_specs = (
        P("off", "tile", None, None),
        P("tile", None, None),
        P("off"),
        P("tile", None),
        P(),
        P(),
        P(),
    )
    out_specs = P("tile", "off", None)
    return jax.shard_map(local, mesh=mesh, in_specs=in_specs, out_specs=out_specs, check_vma=False)
```

time: 43 us -> 35.7 us (0.83)
  local copies, waits for them, and re-layouts: 7.37 us -> 1.24 us
  Pallas kernels: 35.4 us -> 34.3 us
    unnamed x15 -> x1, local copies, waits for them, and re-layouts: 7.37 us -> 1.24 us
    pallas_call x1, Pallas kernels: 35.4 us -> 34.3 us  [local(): pl.pallas_call(kernel, out_shape=jax.ShapeDtypeStruct((2, 1, COARSE), F32...]
where the time goes in v2:
time: 35.7 us; the launch traced here: 35.6 us
  Pallas kernels  34.3 us (96%)
  local copies, waits for them, and re-layouts  1.24 us (3%)
    pallas_call x1, Pallas kernels, local(): pl.pallas_call(kernel, out_shape=jax.ShapeDtypeStruct((2, 1, COARSE), F32...  34.3 us
    unnamed x1, local copies, waits for them, and re-layouts  1.24 us

profile of v2, /device:TPU:1, one launch (start us, length us, event | category | flops | bytes accessed | tf_op | source)
XLA Modules:
  0.0 35.6 jit_solution(279629913459984496)
XLA Ops:
  0.0 34.3 %shard_map.73 = f32[2,1,16]{2,1,0:T(1,128)} custom-call(f32[4,16,128,128]{3,2,1,0:T(8,128)} %cube.1, f32[16,128,128]{2,1,0:T(8,128)} %time.1, s32[1,4]{1,0:T(1,128)} %bitcast.6, f32[16,32]{1,0:T(8,128)} %first.1, f32[16,128]{1,0:T(8,128)} %bitcast.4, f32[16,128]{1,0:T(8,128)} %bitcast.5, s32[1,32]{1,0:T(1,128)} %bitcast.7), custom_call_target="tpu_custom_call" | custom-call | tf_op jit(solution)/shard_map/pallas_call | solution.py:344
  34.3 1.2 %copy.9 = f32[2,1,16]{2,1,0:T(1,128)} copy(f32[2,1,16]{2,1,0:T(1,128)} %shard_map.73) | data formatting | bytes 256

commit v3 on v2

--- a/solution.py
+++ b/solution.py
@@ -21,6 +21,7 @@
 OFFS = 16
 GROUP = 16
 STRIP = 32
+PARTS = [(0, 4), (4, 2), (6, 1), (7, 1)]
 
 
 def iota(shape, axis):
@@ -76,10 +77,22 @@
     has_after = off < OFFS - 1
     has_before = off > 0
 
+    tile_x = [lax.rem(x + dx, 4) * 4 for dx in range(4)]
+    off_y = [lax.rem(y + dy, 4) for dy in range(4)]
+    cores = [core, 1 - core]
+    turned = [lax.rem(z + dz, 8) for dz in range(8)]
+    tile_z = [lax.div(to_z, 4) * 2 for to_z in turned]
+    row_z = [lax.rem(to_z, 4) for to_z in turned]
+    rest_tile, rest_off = z_high * 2 + core, z_low * 4
+    plane_tile = [tile_x[dx] + rest_tile for dx in range(4)]
+    plane_off = [rest_off + off_y[dy] for dy in range(4)]
+    line_tile = [[tile_x[0] + tile_z[dz] + cores[dc] for dc in range(2)] for dz in range(8)]
+    line_off = [row_z[dz] * 4 + y for dz in range(8)]
+
     def around(dx=0, dy=0, dz=0, dc=0):
-        to_x, to_y = lax.rem(x + dx, 4), lax.rem(y + dy, 4)
-        to_z, to_core = lax.rem(z + dz, 8), lax.rem(core + dc, 2)
-        return (to_x * 4 + lax.div(to_z, 4) * 2 + to_core, lax.rem(to_z, 4) * 4 + to_y)
+        if dx or dy:
+            return plane_tile[dx], plane_off[dy]
+        return line_tile[dz][dc], line_off[dz]
 
     def signal(semaphore, device):
         pl.semaphore_signal(semaphore, inc=1, device_id=device, device_id_type=MESH)
@@ -114,15 +127,14 @@
             ]
         )
     ]
-    for load in loads[:5]:
-        load.start()
     extra = turns_after.astype(jnp.int32) + turns_before.astype(jnp.int32)
     pl.semaphore_wait(barrier, len(beside) + extra)
 
     def up(k):
+        start, size = PARTS[k]
         return pltpu.make_async_remote_copy(
-            src_ref=cube.at[LOCAL - 1, HALF + k],
-            dst_ref=before.at[k],
+            src_ref=cube.at[LOCAL - 1, pl.ds(HALF + start, size)],
+            dst_ref=before.at[pl.ds(start, size)],
             send_sem=up_send.at[k],
             recv_sem=up_recv.at[k],
             device_id=(tile, off + 1),
@@ -130,9 +142,10 @@
         )
 
     def down(k):
+        start, size = PARTS[k]
         return pltpu.make_async_remote_copy(
-            src_ref=cube.at[0, k],
-            dst_ref=after.at[k],
+            src_ref=cube.at[0, pl.ds(start, size)],
+            dst_ref=after.at[pl.ds(start, size)],
             send_sem=down_send.at[k],
             recv_sem=down_recv.at[k],
             device_id=(tile, off - 1),
@@ -151,17 +164,17 @@
     @pl.when(has_after)
     def _():
         word.start()
-        for k in range(HALF):
+        for k in range(len(PARTS)):
             up(k).start()
 
     @pl.when(has_before)
     def _():
-        for k in range(HALF):
+        for k in range(len(PARTS)):
             down(k).start()
 
     for d in beside:
         signal(near_sem, around(**d))
-    for load in loads[5:]:
+    for load in loads:
         load.start()
     for load in loads[:5]:
         load.wait()
@@ -246,14 +259,6 @@
     scale_before = pick(theirs * theirs, LOCAL - 1)
 
     def step(k, coarse):
-        @pl.when(has_after)
-        def _():
-            down(k).wait_recv()
-
-        @pl.when(has_before)
-        def _():
-            up(k).wait_recv()
-
         low_rows = time_v[k] * (grad[k] + term(after[k] - cube_v[LOCAL - 1, k], scale[LOCAL - 1]))
         high_rows = time_v[HALF + k] * (
             grad[HALF + k] + term(cube_v[0, HALF + k] - before[k], scale_before)
@@ -274,13 +279,27 @@
         return coarse + (both[:, :WIDE] + both[:, WIDE:])
 
     pl.semaphore_wait(core_sem, 1)
-    coarse = lax.fori_loop(0, HALF, step, jnp.zeros((COARSE, WIDE), F32))
+    coarse = jnp.zeros((COARSE, WIDE), F32)
+    for k, (start, size) in enumerate(PARTS):
+
+        @pl.when(has_after)
+        def _():
+            down(k).wait_recv()
+
+        @pl.when(has_before)
+        def _():
+            up(k).wait_recv()
+
+        if size > 1:
+            coarse = lax.fori_loop(start, start + size, step, coarse)
+        else:
+            coarse = step(start, coarse)
     for to_x in range(4):
         for to_y in range(4):
             send1[to_x * 4 + to_y] = coarse[to_y * 4 : to_y * 4 + 4, to_x * N : (to_x + 1) * N]
 
     def to_plane(dx, dy):
-        index = lax.rem(x + dx, 4) * 4 + lax.rem(y + dy, 4)
+        index = tile_x[dx] + off_y[dy]
         return pltpu.make_async_remote_copy(
             src_ref=send1.at[index],
             dst_ref=recv1.at[dx * 4 + dy],
@@ -300,7 +319,7 @@
         send2[q] = summed[q : q + 1]
 
     def to_line(dz, dc):
-        index = lax.rem(z + dz, 4)
+        index = row_z[dz]
         return pltpu.make_async_remote_copy(
             src_ref=send2.at[index],
             dst_ref=recv2.at[dz * 2 + dc],
@@ -329,12 +348,12 @@
     @pl.when(has_after)
     def _():
         word.wait_send()
-        for k in range(HALF):
+        for k in range(len(PARTS)):
             up(k).wait_send()
 
     @pl.when(has_before)
     def _():
-        for k in range(HALF):
+        for k in range(len(PARTS)):
             down(k).wait_send()
 
 
@@ -365,10 +384,10 @@
             pltpu.VMEM((4, 1, N), F32),
             pltpu.VMEM((GROUP, 1, N), F32),
             dma((7,)),
-            dma((HALF,)),
-            dma((HALF,)),
-            dma((HALF,)),
-            dma((HALF,)),
+            dma((len(PARTS),)),
+            dma((len(PARTS),)),
+            dma((len(PARTS),)),
+            dma((len(PARTS),)),
             dma,
             dma,
             dma,
@@ -380,16 +399,21 @@
             pltpu.SemaphoreType.REGULAR,
         ],
         compiler_params=pltpu.CompilerParams(
-            collective_id=0, has_side_effects=True, vmem_limit_bytes=60 * 1024 * 1024
+            collective_id=0, has_side_effects=True, vmem_limit_bytes=24 * 1024 * 1024
         ),
     )(
-        cube,
-        time,
-        weight.reshape(1, LOCAL),
-        first,
-        second.T,
-        depth.T,
-        owner.reshape(1, FIRST),
+        *(
+            pltpu.with_memory_space_constraint(array, pltpu.HBM)
+            for array in (
+                cube,
+                time,
+                weight.reshape(1, LOCAL),
+                first,
+                second.T,
+                depth.T,
+                owner.reshape(1, FIRST),
+            )
+        )
     )
 
 

time: 35.7 us -> 34.2 us (0.958)
  Pallas kernels: 34.3 us -> 33.5 us
  local copies, waits for them, and re-layouts: 1.24 us -> 0.56 us
    pallas_call x1, Pallas kernels: 34.3 us -> 33.5 us  [local(): pl.pallas_call(kernel, out_shape=jax.ShapeDtypeStruct((2, 1, COARSE), F32...]
    unnamed x1, local copies, waits for them, and re-layouts: 1.24 us -> 0.56 us
where the time goes in v3:
time: 34.2 us; the launch traced here: 34.1 us
  Pallas kernels  33.5 us (98%)
  local copies, waits for them, and re-layouts  0.56 us (2%)
    pallas_call x1, Pallas kernels, local(): pl.pallas_call(kernel, out_shape=jax.ShapeDtypeStruct((2, 1, COARSE), F32...  33.5 us

profile of v3, /device:TPU:1, one launch (start us, length us, event | category | flops | bytes accessed | tf_op | source)
XLA Modules:
  0.0 34.1 jit_solution(17515782224467924874)
XLA Ops:
  0.0 33.5 %shard_map.73 = f32[2,1,16]{2,1,0:T(1,128)S(1)} custom-call(f32[4,16,128,128]{3,2,1,0:T(8,128)} %cube.1, f32[16,128,128]{2,1,0:T(8,128)} %time.1, s32[1,4]{1,0:T(1,128)} %bitcast.6, f32[16,32]{1,0:T(8,128)} %first.1, f32[16,128]{1,0:T(8,128)} %bitcast.4, f32[16,128]{1,0:T(8,128)} %bitcast.5, s32[1,32]{1,0:T(1,128)} %bitcast.7), custom_call_target="tpu_custom_call" | custom-call | tf_op jit(solution)/shard_map/pallas_call | solution.py:363
  33.5 0.6 %copy.9 = f32[2,1,16]{2,1,0:T(1,128)} copy(f32[2,1,16]{2,1,0:T(1,128)S(1)} %shard_map.73) | data formatting | bytes 256

commit v4 on v3

--- a/solution.py
+++ b/solution.py
@@ -21,6 +21,9 @@
 OFFS = 16
 GROUP = 16
 STRIP = 32
+DEVICES = 256
+EARLY = (1, 0)
+KEEP = 64
 PARTS = [(0, 4), (4, 2), (6, 1), (7, 1)]
 
 
@@ -64,10 +67,11 @@
 def kernel(
     cube, time, weight, first, second, depth, owner, out,
     cube_v, time_v, weight_v, first_v, second_v, depth_v, owner_v,
-    before, after, weight_before, grad, chosen, place,
-    send1, recv1, send2, recv2,
+    before, after, rest, weight_before, grad, chosen, place,
+    send1, recv1, send2, recv2, direct_row, direct,
     load_sem, up_send, up_recv, down_send, down_recv, word_send, word_recv,
     s1_send, s1_recv, s2_send, s2_recv, near_sem, far_sem, core_sem,
+    short_send, short_recv, more_send, more_recv, direct_send, direct_recv, early_sem,
 ):
     tile = lax.axis_index("tile")
     off = lax.axis_index("off")
@@ -152,6 +156,28 @@
             device_id_type=MESH,
         )
 
+    last = HALF - 1
+    short = pltpu.make_async_remote_copy(
+        src_ref=cube.at[0, last, pl.ds(0, KEEP)],
+        dst_ref=after.at[last, pl.ds(0, KEEP)],
+        send_sem=short_send,
+        recv_sem=short_recv,
+        device_id=(tile, off - 1),
+        device_id_type=MESH,
+    )
+    more = pltpu.make_async_remote_copy(
+        src_ref=cube.at[LOCAL - 1, last, pl.ds(KEEP, N - KEEP)],
+        dst_ref=rest,
+        send_sem=more_send,
+        recv_sem=more_recv,
+        device_id=(tile, off + 1),
+        device_id_type=MESH,
+    )
+    in_corner = jnp.logical_and(x == 0, y == 0)
+    is_early = jnp.logical_and(tile == EARLY[0], off == EARLY[1])
+    straight_after = jnp.logical_and(has_after, y < 3)
+    straight_before = jnp.logical_and(has_before, y > 0)
+
     word = pltpu.make_async_remote_copy(
         src_ref=weight,
         dst_ref=weight_before,
@@ -164,13 +190,29 @@
     @pl.when(has_after)
     def _():
         word.start()
-        for k in range(len(PARTS)):
+        for k in range(len(PARTS) - 1):
             up(k).start()
 
     @pl.when(has_before)
     def _():
-        for k in range(len(PARTS)):
+        for k in range(len(PARTS) - 1):
             down(k).start()
+
+    @pl.when(turns_after)
+    def _():
+        more.start()
+
+    @pl.when(has_after)
+    def _():
+        up(len(PARTS) - 1).start()
+
+    @pl.when(straight_before)
+    def _():
+        down(len(PARTS) - 1).start()
+
+    @pl.when(turns_before)
+    def _():
+        short.start()
 
     for d in beside:
         signal(near_sem, around(**d))
@@ -279,10 +321,33 @@
         return coarse + (both[:, :WIDE] + both[:, WIDE:])
 
     pl.semaphore_wait(core_sem, 1)
+
+    @pl.when(in_corner)
+    def _():
+        for dx, dy in PLANE:
+            signal(early_sem, around(dx=dx, dy=dy))
+
+    @pl.when(jnp.logical_not(in_corner))
+    def _():
+        pl.semaphore_wait(early_sem, 1)
+
     coarse = jnp.zeros((COARSE, WIDE), F32)
     for k, (start, size) in enumerate(PARTS):
-
-        @pl.when(has_after)
+        if k == len(PARTS) - 1:
+
+            @pl.when(turns_before)
+            def _():
+                more.wait_recv()
+                strip = pl.ds(KEEP, N - KEEP)
+                grad[last, strip, :] += term(cube_v[0, last, strip, :] - rest[...], scale_before)
+
+            @pl.when(turns_after)
+            def _():
+                strip = pl.ds(KEEP, N - KEEP)
+                after[last, strip, :] = cube_v[LOCAL - 1, last, strip, :]
+                short.wait_recv()
+
+        @pl.when(has_after if k < len(PARTS) - 1 else straight_after)
         def _():
             down(k).wait_recv()
 
@@ -294,6 +359,21 @@
             coarse = lax.fori_loop(start, start + size, step, coarse)
         else:
             coarse = step(start, coarse)
+    direct_row[...] = coarse[0:1, 0:N]
+    rank = lax.rem(tile * OFFS + off + DEVICES - (EARLY[0] * OFFS + EARLY[1]), DEVICES)
+    straight = pltpu.make_async_remote_copy(
+        src_ref=direct_row,
+        dst_ref=direct.at[rank],
+        send_sem=direct_send,
+        recv_sem=direct_recv,
+        device_id=EARLY,
+        device_id_type=MESH,
+    )
+
+    @pl.when(jnp.logical_not(is_early))
+    def _():
+        straight.start()
+
     for to_x in range(4):
         for to_y in range(4):
             send1[to_x * 4 + to_y] = coarse[to_y * 4 : to_y * 4 + 4, to_x * N : (to_x + 1) * N]
@@ -329,21 +409,49 @@
             device_id_type=MESH,
         )
 
-    for d in LINE:
-        to_line(*d).start()
-    recv2[0] = send2[z_low]
-    landed = recv2.at[pl.ds(1, GROUP - 1)]
-    pltpu.make_async_copy(landed, landed, s2_recv).wait()
-    result = jnp.sum(recv2[...], axis=0)
-    mine = z_high * 2 + core
-    result = pltpu.roll(result, lax.rem(4 - mine, 4) * (2 * COARSE), 1)
-    for r in range(2):
-        out[r] = result[:, r * COARSE : (r + 1) * COARSE]
+    in_early_line = jnp.logical_and(in_corner, jnp.logical_not(is_early))
+    for dz, dc in LINE:
+        early = jnp.logical_and(turned[dz] == 0, cores[dc] == 1)
+
+        @pl.when(jnp.logical_not(jnp.logical_and(in_corner, early)))
+        def _():
+            to_line(dz, dc).start()
+
+    def finish(rows):
+        mine = z_high * 2 + core
+        result = pltpu.roll(
+            jnp.sum(rows, axis=0), lax.rem(4 - mine, 4) * (2 * COARSE), 1
+        )
+        for r in range(2):
+            out[r] = result[:, r * COARSE : (r + 1) * COARSE]
+
+    @pl.when(is_early)
+    def _():
+        direct[0] = direct_row[...]
+        landed = direct.at[pl.ds(1, DEVICES - 1)]
+        pltpu.make_async_copy(landed, landed, direct_recv).wait()
+        finish(direct[...])
+
+    @pl.when(jnp.logical_not(is_early))
+    def _():
+        recv2[0] = send2[z_low]
+        landed = recv2.at[pl.ds(1, GROUP - 1)]
+        pltpu.make_async_copy(landed, landed, s2_recv).wait()
+        finish(recv2[...])
+        straight.wait_send()
 
     left1 = send1.at[pl.ds(0, GROUP - 1)]
     pltpu.make_async_copy(left1, left1, s1_send).wait()
-    left2 = recv2.at[pl.ds(0, GROUP - 1)]
-    pltpu.make_async_copy(left2, left2, s2_send).wait()
+
+    @pl.when(in_early_line)
+    def _():
+        left2 = recv2.at[pl.ds(0, GROUP - 2)]
+        pltpu.make_async_copy(left2, left2, s2_send).wait()
+
+    @pl.when(jnp.logical_not(in_early_line))
+    def _():
+        left2 = recv2.at[pl.ds(0, GROUP - 1)]
+        pltpu.make_async_copy(left2, left2, s2_send).wait()
 
     @pl.when(has_after)
     def _():
@@ -353,8 +461,20 @@
 
     @pl.when(has_before)
     def _():
-        for k in range(len(PARTS)):
+        for k in range(len(PARTS) - 1):
             down(k).wait_send()
+
+    @pl.when(straight_before)
+    def _():
+        down(len(PARTS) - 1).wait_send()
+
+    @pl.when(turns_before)
+    def _():
+        short.wait_send()
+
+    @pl.when(turns_after)
+    def _():
+        more.wait_send()
 
 
 def local(cube, time, weight, first, second, depth, owner):
@@ -375,6 +495,7 @@
             pltpu.VMEM((1, FIRST), jnp.int32),
             pltpu.VMEM((HALF, N, N), F32),
             pltpu.VMEM((HALF, N, N), F32),
+            pltpu.VMEM((N - KEEP, N), F32),
             pltpu.VMEM((1, LOCAL), jnp.int32),
             pltpu.VMEM((ROWS, N, N), F32),
             pltpu.VMEM((ROWS, WIDE), F32),
@@ -383,6 +504,8 @@
             pltpu.VMEM((GROUP, 4, N), F32),
             pltpu.VMEM((4, 1, N), F32),
             pltpu.VMEM((GROUP, 1, N), F32),
+            pltpu.VMEM((1, N), F32),
+            pltpu.VMEM((DEVICES, 1, N), F32),
             dma((7,)),
             dma((len(PARTS),)),
             dma((len(PARTS),)),
@@ -396,6 +519,13 @@
             dma,
             pltpu.SemaphoreType.REGULAR,
             pltpu.SemaphoreType.REGULAR,
+            pltpu.SemaphoreType.REGULAR,
+            dma,
+            dma,
+            dma,
+            dma,
+            dma,
+            dma,
             pltpu.SemaphoreType.REGULAR,
         ],
         compiler_params=pltpu.CompilerParams(

time: 34.2 us -> 32.1 us (0.939)
  Pallas kernels: 33.5 us -> 31.1 us
    pallas_call x1, Pallas kernels: 33.5 us -> 31.1 us  [local(): pl.pallas_call(kernel, out_shape=jax.ShapeDtypeStruct((2, 1, COARSE), F32...]
where the time goes in v4:
time: 32.1 us; the launch traced here: 31.6 us
  Pallas kernels  31.1 us (97%)
  local copies, waits for them, and re-layouts  0.56 us (2%)
    pallas_call x1, Pallas kernels, local(): pl.pallas_call(kernel, out_shape=jax.ShapeDtypeStruct((2, 1, COARSE), F32...  31.1 us

profile of v4, /device:TPU:1, one launch (start us, length us, event | category | flops | bytes accessed | tf_op | source)
XLA Modules:
  0.0 31.6 jit_solution(9665744723488697587)
XLA Ops:
  0.0 31.1 %shard_map.73 = f32[2,1,16]{2,1,0:T(1,128)S(1)} custom-call(f32[4,16,128,128]{3,2,1,0:T(8,128)} %cube.1, f32[16,128,128]{2,1,0:T(8,128)} %time.1, s32[1,4]{1,0:T(1,128)} %bitcast.6, f32[16,32]{1,0:T(8,128)} %first.1, f32[16,128]{1,0:T(8,128)} %bitcast.4, f32[16,128]{1,0:T(8,128)} %bitcast.5, s32[1,32]{1,0:T(1,128)} %bitcast.7), custom_call_target="tpu_custom_call" | custom-call | tf_op jit(solution)/shard_map/pallas_call | solution.py:483
  31.1 0.6 %copy.9 = f32[2,1,16]{2,1,0:T(1,128)} copy(f32[2,1,16]{2,1,0:T(1,128)S(1)} %shard_map.73) | data formatting | bytes 256

commit v5 on v4

--- a/solution.py
+++ b/solution.py
@@ -22,7 +22,16 @@
 GROUP = 16
 STRIP = 32
 DEVICES = 256
-EARLY = (1, 0)
+EARLY = [
+    ((1, 0), 0, 0),
+    ((0, 4), 1, 0),
+    ((1, 4), 1, 0),
+    ((0, 1), 4, 0),
+    ((1, 1), 4, 0),
+    ((4, 0), 0, 1),
+    ((5, 0), 0, 1),
+]
+EARLY_ROWS = [(0, 0), (1, 0), (4, 0), (0, 1)]
 KEEP = 64
 PARTS = [(0, 4), (4, 2), (6, 1), (7, 1)]
 
@@ -48,6 +57,13 @@
 
 def pick(row, index):
     return jnp.sum(jnp.where(iota(row.shape, 1) == index, row, 0.0), axis=1, keepdims=True)
+
+
+def total(rows):
+    while rows.shape[0] > 1:
+        half = rows.shape[0] // 2
+        rows = rows[:half] + rows[half:]
+    return rows[0]
 
 
 def hops(size, step):
@@ -71,7 +87,7 @@
     send1, recv1, send2, recv2, direct_row, direct,
     load_sem, up_send, up_recv, down_send, down_recv, word_send, word_recv,
     s1_send, s1_recv, s2_send, s2_recv, near_sem, far_sem, core_sem,
-    short_send, short_recv, more_send, more_recv, direct_send, direct_recv, early_sem,
+    short_send, short_recv, more_send, more_recv, direct_send, direct_recv, early_sem, root_sem,
 ):
     tile = lax.axis_index("tile")
     off = lax.axis_index("off")
@@ -174,7 +190,12 @@
         device_id_type=MESH,
     )
     in_corner = jnp.logical_and(x == 0, y == 0)
-    is_early = jnp.logical_and(tile == EARLY[0], off == EARLY[1])
+
+    def early(total, to_core):
+        return jnp.logical_or(total == 1, jnp.logical_and(total == 0, to_core == 1))
+
+    is_early = early(x + y + z, core)
+    is_root = jnp.logical_and(in_corner, jnp.logical_and(z == 0, core == 0))
     straight_after = jnp.logical_and(has_after, y < 3)
     straight_before = jnp.logical_and(has_before, y > 0)
 
@@ -322,6 +343,15 @@
 
     pl.semaphore_wait(core_sem, 1)
 
+    @pl.when(is_root)
+    def _():
+        for dz, dc in LINE:
+            signal(root_sem, around(dz=dz, dc=dc))
+
+    @pl.when(jnp.logical_and(in_corner, jnp.logical_not(is_root)))
+    def _():
+        pl.semaphore_wait(root_sem, 1)
+
     @pl.when(in_corner)
     def _():
         for dx, dy in PLANE:
@@ -359,21 +389,26 @@
             coarse = lax.fori_loop(start, start + size, step, coarse)
         else:
             coarse = step(start, coarse)
-    direct_row[...] = coarse[0:1, 0:N]
-    rank = lax.rem(tile * OFFS + off + DEVICES - (EARLY[0] * OFFS + EARLY[1]), DEVICES)
-    straight = pltpu.make_async_remote_copy(
-        src_ref=direct_row,
-        dst_ref=direct.at[rank],
-        send_sem=direct_send,
-        recv_sem=direct_recv,
-        device_id=EARLY,
-        device_id_type=MESH,
-    )
-
-    @pl.when(jnp.logical_not(is_early))
-    def _():
-        straight.start()
-
+    for i, (row, block) in enumerate(EARLY_ROWS):
+        direct_row[i] = coarse[row : row + 1, block * N : (block + 1) * N]
+
+    def start_straight(target, row, block):
+        to_tile, to_off = target
+        me = tile * OFFS + off
+        there = to_tile * OFFS + to_off
+
+        @pl.when(me != there)
+        def _():
+            pltpu.make_async_remote_copy(
+                src_ref=direct_row.at[EARLY_ROWS.index((row, block))],
+                dst_ref=direct.at[lax.rem(me + DEVICES - there, DEVICES)],
+                send_sem=direct_send,
+                recv_sem=direct_recv,
+                device_id=target,
+                device_id_type=MESH,
+            ).start()
+
+    start_straight(*EARLY[0])
     for to_x in range(4):
         for to_y in range(4):
             send1[to_x * 4 + to_y] = coarse[to_y * 4 : to_y * 4 + 4, to_x * N : (to_x + 1) * N]
@@ -391,10 +426,37 @@
 
     for d in PLANE:
         to_plane(*d).start()
+
+    for target in EARLY[1:]:
+        start_straight(*target)
+
+    @pl.when(has_after)
+    def _():
+        word.wait_send()
+        for k in range(len(PARTS)):
+            up(k).wait_send()
+
+    @pl.when(has_before)
+    def _():
+        for k in range(len(PARTS) - 1):
+            down(k).wait_send()
+
+    @pl.when(straight_before)
+    def _():
+        down(len(PARTS) - 1).wait_send()
+
+    @pl.when(turns_before)
+    def _():
+        short.wait_send()
+
+    @pl.when(turns_after)
+    def _():
+        more.wait_send()
+
     recv1[0] = send1[x * 4 + y]
     landed = recv1.at[pl.ds(1, GROUP - 1)]
     pltpu.make_async_copy(landed, landed, s1_recv).wait()
-    summed = jnp.sum(recv1[...], axis=0)
+    summed = total(recv1[...])
     for q in range(4):
         send2[q] = summed[q : q + 1]
 
@@ -403,34 +465,54 @@
         return pltpu.make_async_remote_copy(
             src_ref=send2.at[index],
             dst_ref=recv2.at[dz * 2 + dc],
-            send_sem=s2_send,
+            send_sem=s2_send.at[dz * 2 + dc],
             recv_sem=s2_recv,
             device_id=around(dz=dz, dc=dc),
             device_id_type=MESH,
         )
 
-    in_early_line = jnp.logical_and(in_corner, jnp.logical_not(is_early))
-    for dz, dc in LINE:
-        early = jnp.logical_and(turned[dz] == 0, cores[dc] == 1)
-
-        @pl.when(jnp.logical_not(jnp.logical_and(in_corner, early)))
+    takes_part = {
+        (dz, dc): jnp.logical_not(early(x + y + turned[dz], cores[dc])) for dz, dc in LINE
+    }
+    for d in LINE:
+
+        @pl.when(takes_part[d])
         def _():
-            to_line(dz, dc).start()
+            to_line(*d).start()
+
+    left1 = send1.at[pl.ds(0, GROUP - 1)]
+    pltpu.make_async_copy(left1, left1, s1_send).wait()
 
     def finish(rows):
         mine = z_high * 2 + core
         result = pltpu.roll(
-            jnp.sum(rows, axis=0), lax.rem(4 - mine, 4) * (2 * COARSE), 1
+            total(rows), lax.rem(4 - mine, 4) * (2 * COARSE), 1
         )
         for r in range(2):
             out[r] = result[:, r * COARSE : (r + 1) * COARSE]
 
+    for d in LINE:
+
+        @pl.when(takes_part[d])
+        def _():
+            to_line(*d).wait_send()
+
     @pl.when(is_early)
     def _():
-        direct[0] = direct_row[...]
+        for i, (row, block) in enumerate(EARLY_ROWS):
+            yours = jnp.logical_and(
+                x == block, jnp.logical_and(y == row // 4, z_low == row % 4)
+            )
+
+            @pl.when(yours)
+            def _():
+                direct[0] = direct_row[i]
+
         landed = direct.at[pl.ds(1, DEVICES - 1)]
         pltpu.make_async_copy(landed, landed, direct_recv).wait()
         finish(direct[...])
+        gone = direct.at[pl.ds(0, len(EARLY) - 1)]
+        pltpu.make_async_copy(gone, gone, direct_send).wait()
 
     @pl.when(jnp.logical_not(is_early))
     def _():
@@ -438,44 +520,8 @@
         landed = recv2.at[pl.ds(1, GROUP - 1)]
         pltpu.make_async_copy(landed, landed, s2_recv).wait()
         finish(recv2[...])
-        straight.wait_send()
-
-    left1 = send1.at[pl.ds(0, GROUP - 1)]
-    pltpu.make_async_copy(left1, left1, s1_send).wait()
-
-    @pl.when(in_early_line)
-    def _():
-        left2 = recv2.at[pl.ds(0, GROUP - 2)]
-        pltpu.make_async_copy(left2, left2, s2_send).wait()
-
-    @pl.when(jnp.logical_not(in_early_line))
-    def _():
-        left2 = recv2.at[pl.ds(0, GROUP - 1)]
-        pltpu.make_async_copy(left2, left2, s2_send).wait()
-
-    @pl.when(has_after)
-    def _():
-        word.wait_send()
-        for k in range(len(PARTS)):
-            up(k).wait_send()
-
-    @pl.when(has_before)
-    def _():
-        for k in range(len(PARTS) - 1):
-            down(k).wait_send()
-
-    @pl.when(straight_before)
-    def _():
-        down(len(PARTS) - 1).wait_send()
-
-    @pl.when(turns_before)
-    def _():
-        short.wait_send()
-
-    @pl.when(turns_after)
-    def _():
-        more.wait_send()
-
+        gone = direct.at[pl.ds(0, len(EARLY))]
+        pltpu.make_async_copy(gone, gone, direct_send).wait()
 
 def local(cube, time, weight, first, second, depth, owner):
     hbm = pl.BlockSpec(memory_space=pltpu.HBM)
@@ -504,7 +550,7 @@
             pltpu.VMEM((GROUP, 4, N), F32),
             pltpu.VMEM((4, 1, N), F32),
             pltpu.VMEM((GROUP, 1, N), F32),
-            pltpu.VMEM((1, N), F32),
+            pltpu.VMEM((len(EARLY_ROWS), 1, N), F32),
             pltpu.VMEM((DEVICES, 1, N), F32),
             dma((7,)),
             dma((len(PARTS),)),
@@ -515,7 +561,7 @@
             dma,
             dma,
             dma,
-            dma,
+            dma((GROUP,)),
             dma,
             pltpu.SemaphoreType.REGULAR,
             pltpu.SemaphoreType.REGULAR,
@@ -526,6 +572,7 @@
             dma,
             dma,
             dma,
+            pltpu.SemaphoreType.REGULAR,
             pltpu.SemaphoreType.REGULAR,
         ],
         compiler_params=pltpu.CompilerParams(

time: 32.1 us -> 31.7 us (0.988); the launches traced: 31.6 us -> 31.6 us
  no operation moved by 1% of the time
where the time goes in v5:
time: 31.7 us; the launch traced here: 31.6 us
  Pallas kernels  31 us (98%)
  local copies, waits for them, and re-layouts  0.56 us (2%)
    pallas_call x1, Pallas kernels, local(): pl.pallas_call(kernel, out_shape=jax.ShapeDtypeStruct((2, 1, COARSE), F32...  31 us

profile of v5, /device:TPU:1, one launch (start us, length us, event | category | flops | bytes accessed | tf_op | source)
XLA Modules:
  0.0 31.6 jit_solution(7834393123923274147)
XLA Ops:
  0.0 31.0 %shard_map.73 = f32[2,1,16]{2,1,0:T(1,128)S(1)} custom-call(f32[4,16,128,128]{3,2,1,0:T(8,128)} %cube.1, f32[16,128,128]{2,1,0:T(8,128)} %time.1, s32[1,4]{1,0:T(1,128)} %bitcast.6, f32[16,32]{1,0:T(8,128)} %first.1, f32[16,128]{1,0:T(8,128)} %bitcast.4, f32[16,128]{1,0:T(8,128)} %bitcast.5, s32[1,32]{1,0:T(1,128)} %bitcast.7), custom_call_target="tpu_custom_call" | custom-call | tf_op jit(solution)/shard_map/pallas_call | solution.py:529
  31.0 0.6 %copy.9 = f32[2,1,16]{2,1,0:T(1,128)} copy(f32[2,1,16]{2,1,0:T(1,128)S(1)} %shard_map.73) | data formatting | bytes 256

commit v6 on v5

--- a/solution.py
+++ b/solution.py
@@ -33,7 +33,7 @@
 ]
 EARLY_ROWS = [(0, 0), (1, 0), (4, 0), (0, 1)]
 KEEP = 64
-PARTS = [(0, 4), (4, 2), (6, 1), (7, 1)]
+PARTS = [(0, 3), (3, 2), (5, 1), (6, 1), (7, 1)]
 
 
 def iota(shape, axis):

time: 31.7 us -> 31.6 us (level)
  no operation moved by 1% of the time
where the time goes in v6:
time: 31.6 us; the launch traced here: 31.4 us
  Pallas kernels  30.9 us (98%)
  local copies, waits for them, and re-layouts  0.56 us (2%)
    pallas_call x1, Pallas kernels, local(): pl.pallas_call(kernel, out_shape=jax.ShapeDtypeStruct((2, 1, COARSE), F32...  30.9 us

profile of v6, /device:TPU:1, one launch (start us, length us, event | category | flops | bytes accessed | tf_op | source)
XLA Modules:
  0.0 31.4 jit_solution(16438116767760161339)
XLA Ops:
  0.0 30.9 %shard_map.73 = f32[2,1,16]{2,1,0:T(1,128)S(1)} custom-call(f32[4,16,128,128]{3,2,1,0:T(8,128)} %cube.1, f32[16,128,128]{2,1,0:T(8,128)} %time.1, s32[1,4]{1,0:T(1,128)} %bitcast.6, f32[16,32]{1,0:T(8,128)} %first.1, f32[16,128]{1,0:T(8,128)} %bitcast.4, f32[16,128]{1,0:T(8,128)} %bitcast.5, s32[1,32]{1,0:T(1,128)} %bitcast.7), custom_call_target="tpu_custom_call" | custom-call | tf_op jit(solution)/shard_map/pallas_call | solution.py:529
  30.9 0.6 %copy.9 = f32[2,1,16]{2,1,0:T(1,128)} copy(f32[2,1,16]{2,1,0:T(1,128)S(1)} %shard_map.73) | data formatting | bytes 256
